TPU v7x, 32 devices: a whole 2x2x4 slice. The times are simulated.
32 devices in a mesh: groups: 2 (over y), dom: 8 (over z, x), feat: 2 (over core).
Axes of the slice: x: 2, y: 2, z: 4, core: 2. Of those that a mesh axis runs over, the one named last changes fastest.
Arguments:
- mesh_nodes: bfloat16 [4096, 512], P(('groups', 'dom'), 'feat'), parts along dimension 0, may hold values from -6 to 6
- mesh_edges: bfloat16 [8192, 512], P(('groups', 'dom'), 'feat'), parts along dimension 0, may hold values from -6 to 6
- grid_nodes: bfloat16 [4096, 512], P(('groups', 'dom'), 'feat'), parts along dimension 0, may hold values from -6 to 6
- decoder_edges: bfloat16 [8192, 512], P(('groups', 'dom'), 'feat'), parts along dimension 0, may hold values from -6 to 6
- mesh_sender: int32 [8192], P(('groups', 'dom')), parts along dimension 0, may hold values from 0 to 271, as said below
- mesh_window: int32 [64], P(('groups', 'dom')), parts along dimension 0, may hold values from 0 to 128
- mesh_segment: int32 [8192], P(('groups', 'dom')), parts along dimension 0, may hold values from 0 to 128, as said below
- mesh_lists: int32 [16, 16], P(('groups', 'dom')), parts along dimension 0, may hold values from 0 to 255
- decoder_sender: int32 [8192], P(('groups', 'dom')), parts along dimension 0, may hold values from 0 to 31, as said below
- decoder_window: int32 [64], P(('groups', 'dom')), parts along dimension 0, may hold values from 0 to 128
- decoder_segment: int32 [8192], P(('groups', 'dom')), parts along dimension 0, may hold values from 0 to 128, as said below
- decoder_lists: int32 [16, 32], P(('groups', 'dom')), parts along dimension 0, may hold values from 0 to 255
- edge_first: bfloat16 [1536, 512], P(None, 'feat'), may hold values from -0.15625 to 0.15625
- edge_second: bfloat16 [512, 512], P('feat'), may hold values from -0.25 to 0.25
- edge_gain: float32 [512], replicated, may hold values from 0.1 to 1.9
- node_first: bfloat16 [1024, 512], P(None, 'feat'), may hold values from -0.1875 to 0.1875
- node_second: bfloat16 [512, 512], P('feat'), may hold values from -0.25 to 0.25
- node_gain: float32 [512], replicated, may hold values from 0.1 to 1.9
- decoder_first: bfloat16 [1536, 512], P(None, 'feat'), may hold values from -0.15625 to 0.15625
- decoder_second: bfloat16 [512, 512], P('feat'), may hold values from -0.25 to 0.25
- decoder_gain: float32 [512], replicated, may hold values from 0.1 to 1.9
- grid_first: bfloat16 [1024, 512], P(None, 'feat'), may hold values from -0.1875 to 0.1875
- grid_second: bfloat16 [512, 512], P('feat'), may hold values from -0.25 to 0.25
- grid_gain: float32 [512], replicated, may hold values from 0.1 to 1.9
Outputs:
- mesh_out: bfloat16 [4096, 512], P(('groups', 'dom'), 'feat'), parts along dimension 0
- grid_out: bfloat16 [4096, 512], P(('groups', 'dom'), 'feat'), parts along dimension 0
There are 2 independent parts, one for each index of `groups`. A program takes and returns all parts, laid end to end along the dimension named above; an argument that names none is the same for every part. Nothing has to cross between parts.
Inputs may be any that keep to these rules, and one draw needn't show every extreme that they name: `mesh_sender`: slots below 256 name an own node of the edge's partition; a slot 256 + q * 2 + c names entry c of what partition q sends to this partition. Every slot is named by some edge of each partition. `mesh_segment`: 128 marks a padding edge; padding edges stand at the end of each partition's rows, and every partition has some. `decoder_sender`: A slot q * 4 + c names entry c of what partition q sends to this slab. Every slot is named by some edge of each slab. `decoder_segment`: 128 marks a padding edge; padding edges stand at the end of each slab's rows, and every slab has some.
All inputs are finite; a program needn't handle non-finite values.
Results may differ from a plain program's by a relative error of at most 0.0052.
Values may be sent and summed in bfloat16 or wider, within the bound.
A program may use at most 64 MiB of HBM per device.

v0:
```python
import jax
import jax.numpy as jnp
from jax import lax
from jax.sharding import PartitionSpec as P

BLOCK = 128


def layer_norm(values, gain):
    average = jnp.mean(values, axis=-1, keepdims=True)
    centered = values - average
    variance = jnp.mean(centered * centered, axis=-1, keepdims=True)
    return centered * lax.rsqrt(variance + 1e-05) * gain


def partial_product(inputs, first, second):
    hidden = jax.nn.silu(jnp.dot(inputs, first, preferred_element_type=jnp.float32)).astype(
        jnp.bfloat16
    )
    return jnp.dot(hidden, second, preferred_element_type=jnp.float32)


def collect_rows(messages, window, segment_ids, node_count):
    receiver = jnp.repeat(window, BLOCK) + segment_ids
    is_live = segment_ids < BLOCK
    node_ids = jnp.arange(node_count, dtype=jnp.int32)
    one_hot = ((receiver[None, :] == node_ids[:, None]) & is_live[None, :]).astype(jnp.bfloat16)
    return jnp.dot(one_hot, messages, preferred_element_type=jnp.float32).astype(jnp.bfloat16)


def local(
    mesh_nodes,
    mesh_edges,
    grid_nodes,
    decoder_edges,
    mesh_sender,
    mesh_window,
    mesh_segment,
    mesh_lists,
    decoder_sender,
    decoder_window,
    decoder_segment,
    decoder_lists,
    edge_first,
    edge_second,
    edge_gain,
    node_first,
    node_second,
    node_gain,
    decoder_first,
    decoder_second,
    decoder_gain,
    grid_first,
    grid_second,
    grid_gain,
):
    split_width = mesh_nodes.shape[1]
    offset = lax.axis_index("feat") * split_width
    mesh_count = mesh_nodes.shape[0]
    grid_count = grid_nodes.shape[0]
    mesh_list = mesh_lists[0]
    decoder_list = decoder_lists[0]
    nodes_full, edges_full = (
        lax.all_gather(mesh_nodes, "feat", axis=1, tiled=True),
        lax.all_gather(mesh_edges, "feat", axis=1, tiled=True),
    )
    outgoing = jnp.take(nodes_full, mesh_list, axis=0)
    arrived = lax.all_to_all(outgoing, "dom", split_axis=0, concat_axis=0, tiled=True)
    lookup_table = jnp.concatenate([nodes_full, arrived], axis=0)
    receiver = jnp.minimum(jnp.repeat(mesh_window, BLOCK) + mesh_segment, mesh_count - 1)
    inputs = jnp.concatenate(
        [
            edges_full,
            jnp.take(lookup_table, mesh_sender, axis=0),
            jnp.take(nodes_full, receiver, axis=0),
        ],
        axis=1,
    )
    edge_terms = partial_product(inputs, edge_first, edge_second)
    summed = lax.psum(edge_terms, "feat")
    message = (edges_full.astype(jnp.float32) + layer_norm(summed, edge_gain)).astype(jnp.bfloat16)
    collected = collect_rows(message, mesh_window, mesh_segment, mesh_count)
    node_inputs = jnp.concatenate([nodes_full, collected], axis=1)
    node_summed = lax.psum(partial_product(node_inputs, node_first, node_second), "feat")
    mesh_full = (nodes_full.astype(jnp.float32) + layer_norm(node_summed, node_gain)).astype(
        jnp.bfloat16
    )
    mesh_out = lax.dynamic_slice_in_dim(mesh_full, offset, split_width, 1)
    sending = jnp.take(mesh_full, decoder_list, axis=0)
    fetched = lax.all_to_all(sending, "dom", split_axis=0, concat_axis=0, tiled=True)
    grid_full, links_full = (
        lax.all_gather(grid_nodes, "feat", axis=1, tiled=True),
        lax.all_gather(decoder_edges, "feat", axis=1, tiled=True),
    )
    grid_receiver = jnp.minimum(jnp.repeat(decoder_window, BLOCK) + decoder_segment, grid_count - 1)
    link_inputs = jnp.concatenate(
        [
            links_full,
            jnp.take(fetched, decoder_sender, axis=0),
            jnp.take(grid_full, grid_receiver, axis=0),
        ],
        axis=1,
    )
    link_terms = partial_product(link_inputs, decoder_first, decoder_second)
    link_summed = lax.psum(link_terms, "feat")
    link_message = (links_full.astype(jnp.float32) + layer_norm(link_summed, decoder_gain)).astype(
        jnp.bfloat16
    )
    arriving = collect_rows(link_message, decoder_window, decoder_segment, grid_count)
    grid_inputs = jnp.concatenate([grid_full, arriving], axis=1)
    grid_summed = lax.psum(partial_product(grid_inputs, grid_first, grid_second), "feat")
    grid_whole = (grid_full.astype(jnp.float32) + layer_norm(grid_summed, grid_gain)).astype(
        jnp.bfloat16
    )
    grid_out = lax.dynamic_slice_in_dim(grid_whole, offset, split_width, 1)
    return (mesh_out, grid_out)


def solution(mesh):
    return jax.shard_map(
        local,
        mesh=mesh,
        in_specs=(
            P(("groups", "dom"), "feat"),
            P(("groups", "dom"), "feat"),
            P(("groups", "dom"), "feat"),
            P(("groups", "dom"), "feat"),
            P(("groups", "dom")),
            P(("groups", "dom")),
            P(("groups", "dom")),
            P(("groups", "dom"), None),
            P(("groups", "dom")),
            P(("groups", "dom")),
            P(("groups", "dom")),
            P(("groups", "dom"), None),
            P(None, "feat"),
            P("feat", None),
            P(),
            P(None, "feat"),
            P("feat", None),
            P(),
            P(None, "feat"),
            P("feat", None),
            P(),
            P(None, "feat"),
            P("feat", None),
            P(),
        ),
        out_specs=(P(("groups", "dom"), "feat"), P(("groups", "dom"), "feat")),
        check_vma=False,
    )
```

profile of v0, /device:TPU:0, one launch (start us, length us, event | category | flops | bytes accessed | tf_op | source)
XLA Modules:
  0.0 154.5 jit_solution(1970100568858117643)
XLA Ops:
  7.2 2.5 %all_gather.12 = bf16[256,512]{1,0:T(8,128)(2,1)S(1)} all-gather(bf16[256,256]{1,0:T(8,128)(2,1)} %param.26), channel_id=1, replica_groups=mesh['groups'=2,'dom'=8,'feat'=2] {'feat'}, dimensions={1}, use_global_device_ids=true | all-gather | bytes 393216 | tf_op jit(solution)/shard_map/all_gather | solution.py:64
  9.7 0.7 fusion.61
  10.4 0.6 gather_fusion
  11.0 0.5 broadcast.237
  11.5 1.3 reduce.6
  12.8 0.1 squeeze.10
  12.9 0.7 broadcast_select_fusion.5
  13.6 7.1 %all-to-all-start = ((bf16[8,2,512]{2,1,0:T(2,128)(2,1)}), bf16[8,2,512]{2,1,0:T(2,128)(2,1)S(1)}, u32[]{:S(2)}, u32[]{:S(2)}) async-start(bf16[8,2,512]{2,1,0:T(2,128)(2,1)} %broadcast_select_fusion.5), calls=%async_computation | async-start | bytes 32768 | tf_op jit(solution)/shard_map/all_to_all | solution.py:68
  20.8 0.0 all-reduce.5.cloned.1.call-start
  20.8 0.7 compare_select_fusion.5
  21.5 0.7 compare_and_fusion.5
  22.2 2.4 %all_gather.13 = bf16[512,512]{1,0:T(8,128)(2,1)S(1)} all-gather(bf16[512,256]{1,0:T(8,128)(2,1)} %param.27), channel_id=1, replica_groups=mesh['groups'=2,'dom'=8,'feat'=2] {'feat'}, dimensions={1}, use_global_device_ids=true | all-gather | bytes 786432 | tf_op jit(solution)/shard_map/all_gather | solution.py:65
  24.6 0.1 compare_and_fusion.3
  24.7 2.0 %gather_fusion.4 = bf16[512,512]{1,0:T(8,128)(2,1)S(1)} fusion(bf16[256,512]{1,0:T(8,128)(2,1)S(1)} %all_gather.12, s32[1024]{0:T(1024)S(1)} %pad_clamp_fusion.3), kind=kCustom, calls=%fused_computation.clone | custom fusion | bytes 1050624 | tf_op jit(solution)/shard_map/jit(_take)/gather | solution.py:75
  26.7 0.1 broadcast_select_fusion.1
  26.8 0.5 copy-done.9
  27.4 0.1 compare_and_fusion.2
  27.5 2.0 %gather_fusion.1 = bf16[512,512]{1,0:T(8,128)(2,1)S(1)} fusion(bf16[272,512]{1,0:T(8,128)(2,1)S(1)} %pad_maximum_fusion, s32[1024]{0:T(1024)S(1)} %pad_clamp_fusion.4), kind=kCustom, calls=%fused_computation.3 | custom fusion | bytes 1050624 | tf_op jit(solution)/shard_map/jit(_take)/gather | solution.py:74
  29.5 0.1 broadcast_select_fusion.3
  29.6 0.8 copy-done.13
  30.4 2.0 %fusion.34 = f32[512,512]{1,0:T(8,128)} fusion(bf16[256,512]{1,0:T(8,128)(2,1)S(1)} %copy-done.13, bf16[1536,256]{1,0:T(8,128)(2,1)S(1)} %copy-done, bf16[512,512]{1,0:T(8,128)(2,1)S(1)} %broadcast_select_fusion.1, bf16[512,512]{1,0:T(8,128)(2,1)S(1)} %broadcast_select_fusion.3, bf16[512,512]{1,0:T(8,128)(2,1)S(1)} %all_gather.13), kind=kOutput, calls=%fused_computation.45 | convolution fusion | flops 542244864 | bytes 3670016 | tf_op jit(solution)/shard_map/dot_general | solution.py:20
  32.4 0.0 all-reduce.5.cloned.1.call-update
  32.5 0.0 all-reduce.7.cloned.1.call-start
  32.5 0.6 copy-done.19
  33.1 0.7 reduce.7
  33.8 0.1 squeeze.12
  33.9 2.2 %all_gather.15 = bf16[512,512]{1,0:T(8,128)(2,1)S(1)} all-gather(bf16[512,256]{1,0:T(8,128)(2,1)S(1)} %copy-done.4), channel_id=1, replica_groups=mesh['groups'=2,'dom'=8,'feat'=2] {'feat'}, dimensions={1}, use_global_device_ids=true | all-gather | bytes 786432 | tf_op jit(solution)/shard_map/all_gather | solution.py:93
  36.1 17.5 %all-reduce.5.cloned.1.call-done = f32[512,512]{1,0:T(8,128)} async-done(((f32[512,512]{1,0:T(8,128)}), f32[512,512]{1,0:T(8,128)}) %all-reduce.5.cloned.1.call-update) | async-done | bytes 1048592 | tf_op jit(solution)/shard_map/psum | solution.py:80
  53.6 1.5 reduce_sum.72
  55.1 0.1 copy-done.2
  55.2 0.3 multiply_reduce_fusion.1
  55.4 1.2 convolution_convert_fusion.1
  56.7 2.5 %fusion.52 = f32[256,512]{1,0:T(8,128)} fusion(bf16[256,512]{1,0:T(8,128)(2,1)S(1)} %copy-done.14, bf16[1024,256]{1,0:T(8,128)(2,1)} %param.41, bf16[256,512]{1,0:T(8,128)(2,1)} %convolution_convert_fusion.1, bf16[256,512]{1,0:T(8,128)(2,1)S(1)} %all_gather.12), kind=kOutput, calls=%fused_computation.63 | convolution fusion | flops 202702848 | bytes 1835008 | tf_op jit(solution)/shard_map/dot_general | solution.py:20
  59.2 0.0 all-reduce.7.cloned.1.call-update
  59.2 2.0 %all_gather.14 = bf16[256,512]{1,0:T(8,128)(2,1)S(1)} all-gather(bf16[256,256]{1,0:T(8,128)(2,1)S(1)} %copy-done.5), channel_id=1, replica_groups=mesh['groups'=2,'dom'=8,'feat'=2] {'feat'}, dimensions={1}, use_global_device_ids=true | all-gather | bytes 393216 | tf_op jit(solution)/shard_map/all_gather | solution.py:92
  61.2 2.0 %gather_fusion.5 = bf16[512,512]{1,0:T(8,128)(2,1)S(1)} fusion(bf16[256,512]{1,0:T(8,128)(2,1)S(1)} %all_gather.14, s32[1024]{0:T(1024)S(1)} %pad_clamp_fusion), kind=kCustom, calls=%fused_computation.1.clone | custom fusion | bytes 1050624 | tf_op jit(solution)/shard_map/jit(_take)/gather | solution.py:100
  63.2 0.1 broadcast_select_fusion
  63.3 15.9 %all-reduce.7.cloned.1.call-done = f32[256,512]{1,0:T(8,128)} async-done(((f32[256,512]{1,0:T(8,128)}), f32[256,512]{1,0:T(8,128)}) %all-reduce.7.cloned.1.call-update) | async-done | bytes 524304 | tf_op jit(solution)/shard_map/psum | solution.py:84
  79.3 1.2 reduce_sum.74
  80.5 1.2 multiply_reduce_fusion.3
  81.8 0.2 add_convert_fusion.4
  81.9 0.6 gather_fusion.2
  82.6 0.7 broadcast_select_fusion.4
  83.3 5.8 %all-to-all-start.1 = ((bf16[8,4,512]{2,1,0:T(4,128)(2,1)}), bf16[8,4,512]{2,1,0:T(4,128)(2,1)S(1)}, u32[]{:S(2)}, u32[]{:S(2)}) async-start(bf16[8,4,512]{2,1,0:T(4,128)(2,1)} %broadcast_select_fusion.4), calls=%async_computation.1 | async-start | bytes 65536 | tf_op jit(solution)/shard_map/all_to_all | solution.py:90
  89.1 0.0 all-reduce.9.cloned.1.call-start
  89.1 6.6 %all-to-all-done.1 = bf16[8,4,512]{2,1,0:T(4,128)(2,1)S(1)} async-done(((bf16[8,4,512]{2,1,0:T(4,128)(2,1)}), bf16[8,4,512]{2,1,0:T(4,128)(2,1)S(1)}, u32[]{:S(2)}, u32[]{:S(2)}) %all-to-all-start.1) | async-done | bytes 32800 | tf_op jit(solution)/shard_map/all_to_all | solution.py:90
  95.8 2.0 %gather_fusion.3 = bf16[512,512]{1,0:T(8,128)(2,1)S(1)} fusion(bf16[32,512]{1,0:T(8,128)(2,1)S(1)} %all_to_all.15, s32[1024]{0:T(1024)S(1)} %pad_clamp_fusion.1), kind=kCustom, calls=%fused_computation.5 | custom fusion | bytes 1050624 | tf_op jit(solution)/shard_map/jit(_take)/gather | solution.py:99
  97.8 1.0 broadcast_select_fusion.2
  98.7 3.3 %fusion.26 = f32[512,512]{1,0:T(8,128)} fusion(bf16[256,512]{1,0:T(8,128)(2,1)S(1)} %copy-done.15, bf16[1536,256]{1,0:T(8,128)(2,1)} %param.44, bf16[512,512]{1,0:T(8,128)(2,1)S(1)} %broadcast_select_fusion, bf16[512,512]{1,0:T(8,128)(2,1)} %broadcast_select_fusion.2, bf16[512,512]{1,0:T(8,128)(2,1)S(1)} %all_gather.15), kind=kOutput, calls=%fused_computation.37 | convolution fusion | flops 542244864 | bytes 3670016 | tf_op jit(solution)/shard_map/dot_general | solution.py:20
  102.0 0.0 all-reduce.9.cloned.1.call-update
  102.0 0.0 all-reduce.11.cloned.1.call-start
  102.1 17.1 %all-reduce.9.cloned.1.call-done = f32[512,512]{1,0:T(8,128)} async-done(((f32[512,512]{1,0:T(8,128)}), f32[512,512]{1,0:T(8,128)}) %all-reduce.9.cloned.1.call-update) | async-done | bytes 1048592 | tf_op jit(solution)/shard_map/psum | solution.py:105
  119.1 1.5 reduce_sum.76
  120.6 0.1 copy-done.3
  120.7 0.3 multiply_reduce_fusion
  121.0 1.2 convolution_convert_fusion
  122.2 2.5 %fusion.46 = f32[256,512]{1,0:T(8,128)} fusion(bf16[256,512]{1,0:T(8,128)(2,1)S(1)} %copy-done.16, bf16[1024,256]{1,0:T(8,128)(2,1)} %param.47, bf16[256,512]{1,0:T(8,128)(2,1)} %convolution_convert_fusion, bf16[256,512]{1,0:T(8,128)(2,1)S(1)} %all_gather.14), kind=kOutput, calls=%fused_computation.60 | convolution fusion | flops 202702848 | bytes 1835008 | tf_op jit(solution)/shard_map/dot_general | solution.py:20
  124.6 0.0 all-reduce.11.cloned.1.call-update
  124.7 0.1 dynamic-slice
  124.8 0.7 constant_dynamic-slice_fusion
  125.4 19.3 %all-reduce.11.cloned.1.call-done = f32[256,512]{1,0:T(8,128)} async-done(((f32[256,512]{1,0:T(8,128)}), f32[256,512]{1,0:T(8,128)}) %all-reduce.11.cloned.1.call-update) | async-done | bytes 524304 | tf_op jit(solution)/shard_map/psum | solution.py:111
  144.7 1.2 reduce_sum.78
  145.9 1.2 multiply_reduce_fusion.2
  147.2 0.8 fusion.42
  (62 shorter events, 0.3 us)
Async XLA Ops:
  7.2 22.5 %copy-start = (bf16[1536,256]{1,0:T(8,128)(2,1)S(1)}, bf16[1536,256]{1,0:T(8,128)(2,1)}, u32[]{:S(2)}) copy-start(bf16[1536,256]{1,0:T(8,128)(2,1)} %param.38) | copy-start | bytes 2359300
  7.2 17.4 %copy-start.8 = (s32[512]{0:T(512)S(1)}, s32[512]{0:T(512)}, u32[]{:S(2)}) copy-start(s32[512]{0:T(512)} %param.32) | copy-start | bytes 6148
  7.2 17.4 %copy-start.11 = (s32[4]{0:T(128)S(1)}, s32[4]{0:T(128)}, u32[]{:S(2)}) copy-start(s32[4]{0:T(128)} %param.31) | copy-start | bytes 52
  13.6 13.8 %all-to-all-start = ((bf16[8,2,512]{2,1,0:T(2,128)(2,1)}), bf16[8,2,512]{2,1,0:T(2,128)(2,1)S(1)}, u32[]{:S(2)}, u32[]{:S(2)}) async-start(bf16[8,2,512]{2,1,0:T(2,128)(2,1)} %broadcast_select_fusion.5), calls=%async_computation | async-start | bytes 32768 | tf_op jit(solution)/shard_map/all_to_all | solution.py:68
  20.8 32.8 %all-reduce.5.cloned.1.call-start = ((), (), s32[]{:S(2)}) async-start(), calls=%async_computation.2 | async-start | bytes 2097152 | tf_op jit(solution)/shard_map/psum | solution.py:80
  26.7 0.7 copy-start.9
  26.7 0.7 copy-start.12
  29.5 1.0 copy-start.13
  32.4 0.7 copy-start.19
  32.4 1.4 copy-start.4
  32.4 3.6 %copy-start.6 = (s32[512]{0:T(512)S(1)}, s32[512]{0:T(512)}, u32[]{:S(2)}) copy-start(s32[512]{0:T(512)} %param.34) | copy-start | bytes 6148
  32.5 46.8 %all-reduce.7.cloned.1.call-start = ((), (), s32[]{:S(2)}) async-start(), calls=%async_computation.3 | async-start | bytes 1048576 | tf_op jit(solution)/shard_map/psum | solution.py:84
  36.1 19.3 %copy-start.17 = (f32[512]{0:T(512)S(1)}, f32[512]{0:T(512)}, u32[]{:S(2)}) copy-start(f32[512]{0:T(512)} %param.40) | copy-start | bytes 6148
  53.6 1.5 copy-start.2
  55.4 1.2 copy-start.14
  56.6 2.5 %copy-start.5 = (bf16[256,256]{1,0:T(8,128)(2,1)S(1)}, bf16[256,256]{1,0:T(8,128)(2,1)}, u32[]{:S(2)}) copy-start(bf16[256,256]{1,0:T(8,128)(2,1)} %param.28) | copy-start | bytes 393220
  63.2 18.6 %copy-start.7 = (f32[512]{0:T(512)S(1)}, f32[512]{0:T(512)}, u32[]{:S(2)}) copy-start(f32[512]{0:T(512)} %param.43) | copy-start | bytes 6148
  79.2 2.5 %copy-start.1 = (f32[256,512]{1,0:T(8,128)S(1)}, f32[256,512]{1,0:T(8,128)}, u32[]{:S(2)}) copy-start(f32[256,512]{1,0:T(8,128)} %all-reduce.7.cloned.1.call-done) | copy-start | bytes 1572868
  83.3 12.5 %all-to-all-start.1 = ((bf16[8,4,512]{2,1,0:T(4,128)(2,1)}), bf16[8,4,512]{2,1,0:T(4,128)(2,1)S(1)}, u32[]{:S(2)}, u32[]{:S(2)}) async-start(bf16[8,4,512]{2,1,0:T(4,128)(2,1)} %broadcast_select_fusion.4), calls=%async_computation.1 | async-start | bytes 65536 | tf_op jit(solution)/shard_map/all_to_all | solution.py:90
  89.1 30.0 %all-reduce.9.cloned.1.call-start = ((), (), s32[]{:S(2)}) async-start(), calls=%async_computation.4 | async-start | bytes 2097152 | tf_op jit(solution)/shard_map/psum | solution.py:105
  97.8 1.0 copy-start.15
  102.0 18.9 %copy-start.18 = (f32[512]{0:T(512)S(1)}, f32[512]{0:T(512)}, u32[]{:S(2)}) copy-start(f32[512]{0:T(512)} %param.46) | copy-start | bytes 6148
  102.0 42.7 %all-reduce.11.cloned.1.call-start = ((), (), s32[]{:S(2)}) async-start(), calls=%async_computation.5 | async-start | bytes 1048576 | tf_op jit(solution)/shard_map/psum | solution.py:111
  119.1 1.5 copy-start.3
  120.9 1.2 copy-start.16
  122.2 2.5 %copy-start.10 = (f32[512]{0:T(512)S(1)}, f32[512]{0:T(512)}, u32[]{:S(2)}) copy-start(f32[512]{0:T(512)} %param.49) | copy-start | bytes 6148
Sparse Core Ops, SparseCore 0:
  32.6 20.9 all-reduce.4
  59.3 19.9 all-reduce.6
  102.1 16.9 all-reduce.8
  124.8 19.9 all-reduce.10
where the time goes:
time: 155 us; the launch traced here: 154 us
  waiting for transfers between devices  76.5 us (49%)
  other arithmetic  16.3 us (11%)
  between operations  14.2 us (9%)
  starting transfers between devices  13.1 us (8%)
  local copies, waits for them, and re-layouts  12.7 us (8%)
  matrix products  12.7 us (8%)
  blocking collectives  9.09 us (6%)
    psum x1, waiting for transfers between devices, local(): lax.psum(partial_product(grid_inputs, grid_first, grid_second), 'feat')  19.3 us
    psum x1, waiting for transfers between devices, local(): summed = lax.psum(edge_terms, 'feat')  17.5 us
    psum x1, waiting for transfers between devices, local(): link_summed = lax.psum(link_terms, 'feat')  17.1 us
    psum x1, waiting for transfers between devices, local(): lax.psum(partial_product(node_inputs, node_first, node_second), 'feat')  15.9 us
    dot_general x4, matrix products, partial_product(): return jnp.dot(hidden, second, preferred_element_type=jnp.float32)  10.2 us
    all_to_all x1, starting transfers between devices, local(): lax.all_to_all(outgoing, 'dom', split_axis=0, concat_axis=0, tiled=True)  7.15 us
    all_to_all x1, waiting for transfers between devices, local(): lax.all_to_all(sending, 'dom', split_axis=0, concat_axis=0, tiled=True)  6.63 us
    all_to_all x1, starting transfers between devices, local(): lax.all_to_all(sending, 'dom', split_axis=0, concat_axis=0, tiled=True)  5.78 us
  transfers between devices with their start and end apart: 6, of which 5 were waited for; matrix products, arithmetic and copies ran while one was open for 5% of the time, Pallas kernels for 0%

commit v1 on v0

v1 whole, which is shorter than its diff:
```python
import functools

import jax
import jax.numpy as jnp
from jax import lax
from jax.experimental import pallas as pl
from jax.experimental.pallas import tpu as pltpu
from jax.sharding import PartitionSpec as P

BLOCK = 128
LANES = 128
SLOT = 16
MESH = pl.DeviceIdType.MESH
F32 = jnp.float32
BF16 = jnp.bfloat16


def dot(a, b):
    return jnp.dot(a, b, preferred_element_type=F32)


def silu(v):
    half = 0.5 * v
    return (half * jnp.tanh(half) + half).astype(BF16)


def norm_scale(values):
    average = jnp.mean(values, axis=-1, keepdims=True)
    centered = values - average
    variance = jnp.mean(centered * centered, axis=-1, keepdims=True)
    return centered * lax.rsqrt(variance + 1e-05)


def every(count, body):
    if count <= 16:
        for i in range(count):
            body(i)
    else:

        def step(i, carry):
            body(i)
            return carry

        lax.fori_loop(0, count, step, 0)


def iota(shape, dim):
    return lax.broadcasted_iota(jnp.int32, shape, dim)


def kernel(n, *refs):
    (
        nodes_in, edges_in, grid_in, links_in,
        sender_in, window_ref, segment_in, lists_in,
        dsender_in, dwindow_ref, dsegment_in, dlists_in,
        ef_in, es_in, eg_in, nf_in, ns_in, ng_in,
        df_in, ds_in, dg_in, gf_in, gs_in, gg_in,
        mesh_out, grid_out,
        nodes, edges, grid, links,
        sender, segment, lists, dsender, dsegment, dlists,
        ef, es, eg, nf, ns, ng, df, ds, dg, gf, gs, gg,
        send1, recv1, send2, recv2, mesh_full, grid_full,
        local_sem, feat_send, feat_recv, small_sem,
        a_send, a_recv, b_send, b_recv, out_sem,
    ) = refs
    me = lax.axis_index("dom")
    core = lax.axis_index("feat")
    other = 1 - core
    width = nodes_in.shape[1]
    mesh_count = nodes_in.shape[0]
    grid_count = grid_in.shape[0]
    edge_count = edges_in.shape[0]
    latent = 2 * width
    chunks = latent // LANES

    def column_half(ref, c):
        return ref.at[:, pl.ds(pl.multiple_of(c * width, width), width)]

    def row_half(ref, c):
        return ref.at[pl.ds(pl.multiple_of(c * width, width), width), :]

    barrier = pltpu.get_barrier_semaphore()
    pl.semaphore_signal(barrier, inc=1, device_id={"feat": other}, device_id_type=MESH)
    every(
        n - 1,
        lambda i: pl.semaphore_signal(
            barrier, inc=1, device_id={"dom": lax.rem(me + i + 1, n)}, device_id_type=MESH
        ),
    )

    shared = (
        (nodes_in, nodes, column_half),
        (ef_in, ef, column_half),
        (edges_in, edges, column_half),
        (es_in, es, row_half),
        (nf_in, nf, column_half),
        (ns_in, ns, row_half),
        (links_in, links, column_half),
        (grid_in, grid, column_half),
        (df_in, df, column_half),
        (ds_in, ds, row_half),
        (gf_in, gf, column_half),
        (gs_in, gs, row_half),
    )
    small = (
        (sender_in, sender), (segment_in, segment), (lists_in, lists),
        (dsender_in, dsender), (dsegment_in, dsegment), (dlists_in, dlists),
        (eg_in, eg), (ng_in, ng), (dg_in, dg), (gg_in, gg),
    )
    own = []
    far = []
    for i, (src, dst, half) in enumerate(shared):
        own.append(pltpu.make_async_copy(src, half(dst, core), local_sem.at[i]))
        far.append(
            pltpu.make_async_remote_copy(
                src_ref=src,
                dst_ref=half(dst, core),
                send_sem=feat_send.at[i],
                recv_sem=feat_recv.at[i],
                device_id={"feat": other},
                device_id_type=MESH,
            )
        )
    near = [
        pltpu.make_async_copy(src, dst, small_sem.at[i]) for i, (src, dst) in enumerate(small)
    ]
    own[0].start()
    for copy in near:
        copy.start()
    for copy in own[1:]:
        copy.start()
    pl.semaphore_wait(barrier, n)
    for copy in far:
        copy.start()

    def arrived(*which):
        for i in which:
            own[i].wait()
            far[i].wait_recv()

    def exchange(send, recv, send_sem, recv_sem, where, at):
        return pltpu.make_async_remote_copy(
            src_ref=send.at[where],
            dst_ref=recv.at[at],
            send_sem=send_sem.at[where],
            recv_sem=recv_sem.at[at],
            device_id={"dom": where},
            device_id_type=MESH,
        )

    def send_listed(table, list_row, send, recv, send_sem, recv_sem):
        cap = list_row.shape[1] // n
        rows = n * SLOT
        shape = (rows, n * cap)
        r = iota(shape, 0)
        wanted = (r // SLOT) * cap + r % cap
        picked = jnp.sum(
            jnp.where(iota(shape, 1) == wanted, list_row, 0).astype(F32), axis=1, keepdims=True
        ).astype(jnp.int32)
        one_hot = (iota((rows, mesh_count), 1) == picked).astype(BF16)
        whole = dot(one_hot, table)
        chunk = (iota((rows, LANES), 0) % SLOT) // cap
        packed = jnp.zeros((rows, LANES), F32)
        for j in range(chunks):
            packed = jnp.where(chunk == j, whole[:, j * LANES : (j + 1) * LANES], packed)
        packed = packed.astype(BF16).reshape(n, SLOT, LANES)
        send[...] = packed
        every(
            n - 1,
            lambda i: exchange(
                send, recv, send_sem, recv_sem, lax.rem(me + i + 1, n), me
            ).start(),
        )
        recv[me] = send[me]

    def receive_listed(recv, send, send_sem, recv_sem, cap, weights):
        def wait(i):
            q = lax.rem(me + i + 1, n)
            exchange(send, recv, send_sem, recv_sem, q, q).wait_recv()

        every(n - 1, wait)
        rows = n * SLOT
        packed = recv[...].reshape(rows, LANES).astype(F32)
        chunk = (iota((rows, LANES), 0) % SLOT) // cap
        spread = jnp.concatenate(
            [jnp.where(chunk == j, packed, 0.0) for j in range(chunks)], axis=1
        ).astype(BF16)
        return dot(spread, weights).astype(BF16)

    def slot_key(cap):
        r = iota((1, n * SLOT), 1)
        key = (r // SLOT) * cap + r % cap
        return jnp.where(r % SLOT < chunks * cap, key, -1)

    for copy in near:
        copy.wait()

    def receivers(segment_row, window):
        lane_block = iota((1, edge_count), 1) // BLOCK
        first = jnp.zeros((1, edge_count), jnp.int32)
        for k in range(edge_count // BLOCK):
            first = jnp.where(lane_block == k, window[k], first)
        return jnp.where(segment_row < BLOCK, first + segment_row, -1)

    receiver = receivers(segment[...], window_ref)
    dreceiver = receivers(dsegment[...], dwindow_ref)
    which = iota((8, edge_count), 0)
    rows = jnp.where(
        which == 0,
        sender[...],
        jnp.where(which == 1, receiver, jnp.where(which == 2, dsender[...], dreceiver)),
    )
    columns = rows.astype(F32).T.astype(jnp.int32)
    sender_col, receiver_col = columns[:, 0:1], columns[:, 1:2]
    dsender_col, dreceiver_col = columns[:, 2:3], columns[:, 3:4]

    arrived(0)
    send_listed(nodes[...], lists[...], send1, recv1, a_send, a_recv)

    mesh_cap = lists_in.shape[1] // n
    grid_cap = dlists_in.shape[1] // n
    arrived(1)
    from_sender = dot(nodes[...], ef[latent : 2 * latent, :]).astype(BF16)
    from_receiver = dot(nodes[...], ef[2 * latent : 3 * latent, :]).astype(BF16)
    node_lane = iota((edge_count, mesh_count), 1)
    pick_sender = (node_lane == sender_col).astype(BF16)
    pick_receiver = (node_lane == receiver_col).astype(BF16)
    pre = dot(pick_sender, from_sender) + dot(pick_receiver, from_receiver)
    arrived(2)
    pre = pre + dot(edges[...], ef[0:latent, :])
    table = receive_listed(recv1, send1, a_send, a_recv, mesh_cap, ef[latent : 2 * latent, :])
    pick_slot = (slot_key(mesh_cap) == sender_col - mesh_count).astype(BF16)
    hidden = silu(pre + dot(pick_slot, table))
    arrived(3)
    message = (
        edges[...].astype(F32) + norm_scale(dot(hidden, es[...])) * eg[...]
    ).astype(BF16)
    gather = (iota((mesh_count, edge_count), 0) == receiver).astype(BF16)
    collected = dot(gather, message).astype(BF16)

    arrived(4)
    hidden = silu(dot(nodes[...], nf[0:latent, :]) + dot(collected, nf[latent : 2 * latent, :]))
    arrived(5)
    updated = (nodes[...].astype(F32) + norm_scale(dot(hidden, ns[...])) * ng[...]).astype(BF16)
    mesh_full[...] = updated
    send_listed(updated, dlists[...], send2, recv2, b_send, b_recv)
    put_mesh = pltpu.make_async_copy(column_half(mesh_full, core), mesh_out, out_sem.at[0])
    put_mesh.start()

    arrived(6, 7, 8)
    from_grid = dot(grid[...], df[2 * latent : 3 * latent, :]).astype(BF16)
    grid_lane = iota((edge_count, grid_count), 1)
    pick_grid = (grid_lane == dreceiver_col).astype(BF16)
    pre = dot(links[...], df[0:latent, :]) + dot(pick_grid, from_grid)
    arrived(10)
    grid_pre = dot(grid[...], gf[0:latent, :])
    table = receive_listed(recv2, send2, b_send, b_recv, grid_cap, df[latent : 2 * latent, :])
    pick_slot = (slot_key(grid_cap) == dsender_col).astype(BF16)
    hidden = silu(pre + dot(pick_slot, table))
    arrived(9)
    message = (
        links[...].astype(F32) + norm_scale(dot(hidden, ds[...])) * dg[...]
    ).astype(BF16)
    gather = (iota((grid_count, edge_count), 0) == dreceiver).astype(BF16)
    collected = dot(gather, message).astype(BF16)

    hidden = silu(grid_pre + dot(collected, gf[latent : 2 * latent, :]))
    arrived(11)
    grid_full[...] = (
        grid[...].astype(F32) + norm_scale(dot(hidden, gs[...])) * gg[...]
    ).astype(BF16)
    put_grid = pltpu.make_async_copy(column_half(grid_full, core), grid_out, out_sem.at[1])
    put_grid.start()

    for copy in far:
        copy.wait_send()

    def sent(i):
        q = lax.rem(me + i + 1, n)
        exchange(send1, recv1, a_send, a_recv, q, q).wait_send()
        exchange(send2, recv2, b_send, b_recv, q, q).wait_send()

    every(n - 1, sent)
    put_mesh.wait()
    put_grid.wait()


def local(n, *args):
    args = list(args)
    for i in (4, 6, 8, 10, 14, 17, 20, 23):
        args[i] = args[i].reshape(1, -1)
    width = args[0].shape[1]
    latent = 2 * width
    any_spec = pl.BlockSpec(memory_space=pl.ANY)
    smem = pl.BlockSpec(memory_space=pltpu.SMEM)
    in_specs = [any_spec] * len(args)
    in_specs[5] = smem
    in_specs[9] = smem

    def whole_columns(a):
        return pltpu.VMEM((a.shape[0], latent), a.dtype)

    def whole_rows(a):
        return pltpu.VMEM((latent, a.shape[1]), a.dtype)

    def same(a):
        return pltpu.VMEM(a.shape, a.dtype)

    slots = pltpu.VMEM((n, SLOT, LANES), BF16)
    dma = pltpu.SemaphoreType.DMA
    return pl.pallas_call(
        functools.partial(kernel, n),
        out_shape=(
            jax.ShapeDtypeStruct(args[0].shape, BF16),
            jax.ShapeDtypeStruct(args[2].shape, BF16),
        ),
        in_specs=in_specs,
        out_specs=(any_spec, any_spec),
        scratch_shapes=[
            *[whole_columns(a) for a in args[0:4]],
            *[same(args[i]) for i in (4, 6, 7, 8, 10, 11)],
            whole_columns(args[12]), whole_rows(args[13]), same(args[14]),
            whole_columns(args[15]), whole_rows(args[16]), same(args[17]),
            whole_columns(args[18]), whole_rows(args[19]), same(args[20]),
            whole_columns(args[21]), whole_rows(args[22]), same(args[23]),
            slots, slots, slots, slots,
            whole_columns(args[0]), whole_columns(args[2]),
            dma((12,)), dma((12,)), dma((12,)), dma((10,)),
            dma((n,)), dma((n,)), dma((n,)), dma((n,)), dma((2,)),
        ],
        compiler_params=pltpu.CompilerParams(
            collective_id=0, has_side_effects=True, vmem_limit_bytes=56 * 1024 * 1024
        ),
        name="layer",
    )(*args)


def solution(mesh):
    rows = P(("groups", "dom"))
    split = P(("groups", "dom"), "feat")
    first, second, gain = P(None, "feat"), P("feat", None), P()
    return jax.shard_map(
        functools.partial(local, mesh.shape["dom"]),
        mesh=mesh,
        in_specs=(
            split, split, split, split,
            rows, rows, rows, P(("groups", "dom"), None),
            rows, rows, rows, P(("groups", "dom"), None),
            first, second, gain,
            first, second, gain,
            first, second, gain,
            first, second, gain,
        ),
        out_specs=(split, split),
        check_vma=False,
    )
```

time: 155 us -> 25.2 us (0.16)
  waiting for transfers between devices: 76.5 us -> 0 us
  Pallas kernels: 0 us -> 22.1 us
  other arithmetic: 16.3 us -> 0 us
  between operations: 14.2 us -> 0.66 us
  starting transfers between devices: 13.1 us -> 0 us
  matrix products: 12.7 us -> 0 us
  local copies, waits for them, and re-layouts: 12.7 us -> 2.26 us
  blocking collectives: 9.09 us -> 0 us
    psum x4 -> x0, waiting for transfers between devices: 69.8 us -> none  [the longest x1 19.3 us: local(): lax.psum(partial_product(grid_inputs, grid_first, grid_second), 'feat')]
    pallas_call x0 -> x1, Pallas kernels: none -> 22.1 us  [local(): pl.pallas_call(functools.partial(kernel, n), out_shape=(jax.ShapeDtypeStr...]
    all_to_all x2 -> x0, starting transfers between devices: 12.9 us -> none  [the longest x1 7.15 us: local(): lax.all_to_all(outgoing, 'dom', split_axis=0, concat_axis=0, tiled=True)]
    dot_general x6 -> x0, matrix products: 12.7 us -> none  [the longest x4 10.2 us: partial_product(): return jnp.dot(hidden, second, preferred_element_type=jnp.float32)]
    gather x8 -> x0, local copies, waits for them, and re-layouts: 9.12 us -> none  [the longest x1 1.97 us: local(): jnp.take(nodes_full, receiver, axis=0)]
    all_gather x4 -> x0, blocking collectives: 9.09 us -> none  [the longest x1 2.54 us: local(): lax.all_gather(mesh_nodes, 'feat', axis=1, tiled=True)]
    reduce_sum x8 -> x0, other arithmetic: 8.28 us -> none  [the longest x4 5.3 us: layer_norm(): average = jnp.mean(values, axis=-1, keepdims=True)]
    all_to_all x2 -> x0, waiting for transfers between devices: 6.63 us -> none  [the longest x1 6.63 us: local(): lax.all_to_all(sending, 'dom', split_axis=0, concat_axis=0, tiled=True)]
  transfers between devices with their start and end apart: 6 -> 0, of which waited for: 5 -> 0; matrix products, arithmetic and copies ran while one was open for 5% -> 0% of each run, Pallas kernels for 0% -> 0%
where the time goes in v1:
time: 25.2 us; the launch traced here: 25 us
  Pallas kernels  22.1 us (88%)
  local copies, waits for them, and re-layouts  2.26 us (9%)
  between operations  0.66 us (3%)
    pallas_call x1, Pallas kernels, local(): pl.pallas_call(functools.partial(kernel, n), out_shape=(jax.ShapeDtypeStr...  22.1 us
    unnamed x4, local copies, waits for them, and re-layouts  2.26 us

profile of v1, /device:TPU:0, one launch (start us, length us, event | category | flops | bytes accessed | tf_op | source)
XLA Modules:
  0.0 25.0 jit_solution(945851100656831232)
XLA Ops:
  0.6 22.1 %layer.1 = (bf16[256,256]{1,0:T(8,128)(2,1)}, bf16[256,256]{1,0:T(8,128)(2,1)}) custom-call(bf16[256,256]{1,0:T(8,128)(2,1)} %refs_0_.1, bf16[512,256]{1,0:T(8,128)(2,1)} %refs_1_.1, bf16[256,256]{1,0:T(8,128)(2,1)} %refs_2_.1, bf16[512,256]{1,0:T(8,128)(2,1)} %refs_3_.1, s32[1,512]{1,0:T(1,128)} %bitcast.8, s32[4]{0:T(128)} %refs_5_.1, s32[1,512]{1,0:T(1,128)} %bitcast.9, ...), custom_call_target="tpu_custom_call" | custom-call | tf_op jit(solution)/shard_map/layer/pallas_call | solution.py:311
  22.7 0.0 copy-start
  22.7 1.6 %copy.28 = bf16[256,256]{1,0:T(8,128)(2,1)} copy(bf16[256,256]{1,0:T(8,128)(2,1)} %get-tuple-element.4) | data formatting | bytes 262144
  24.3 0.0 copy-done
  24.3 0.7 %copy.29 = bf16[256,256]{1,0:T(8,128)(2,1)} copy(bf16[256,256]{1,0:T(8,128)(2,1)S(1)} %copy-done) | data formatting | bytes 262144
Async XLA Ops:
  22.7 1.6 %copy-start = (bf16[256,256]{1,0:T(8,128)(2,1)S(1)}, bf16[256,256]{1,0:T(8,128)(2,1)}, u32[]{:S(2)}) copy-start(bf16[256,256]{1,0:T(8,128)(2,1)} %get-tuple-element.5) | copy-start | bytes 393220

commit v2 on v1

--- a/solution.py
+++ b/solution.py
@@ -81,12 +81,17 @@
 
     barrier = pltpu.get_barrier_semaphore()
     pl.semaphore_signal(barrier, inc=1, device_id={"feat": other}, device_id_type=MESH)
-    every(
-        n - 1,
-        lambda i: pl.semaphore_signal(
-            barrier, inc=1, device_id={"dom": lax.rem(me + i + 1, n)}, device_id_type=MESH
-        ),
-    )
+
+    def greet(i):
+        for c in range(2):
+            pl.semaphore_signal(
+                barrier,
+                inc=1,
+                device_id={"dom": lax.rem(me + i + 1, n), "feat": c},
+                device_id_type=MESH,
+            )
+
+    every(n - 1, greet)
 
     shared = (
         (nodes_in, nodes, column_half),
@@ -129,9 +134,6 @@
         copy.start()
     for copy in own[1:]:
         copy.start()
-    pl.semaphore_wait(barrier, n)
-    for copy in far:
-        copy.start()
 
     def arrived(*which):
         for i in which:
@@ -148,7 +150,7 @@
             device_id_type=MESH,
         )
 
-    def send_listed(table, list_row, send, recv, send_sem, recv_sem):
+    def listed_rows(list_row):
         cap = list_row.shape[1] // n
         rows = n * SLOT
         shape = (rows, n * cap)
@@ -157,35 +159,36 @@
         picked = jnp.sum(
             jnp.where(iota(shape, 1) == wanted, list_row, 0).astype(F32), axis=1, keepdims=True
         ).astype(jnp.int32)
-        one_hot = (iota((rows, mesh_count), 1) == picked).astype(BF16)
-        whole = dot(one_hot, table)
+        return (iota((rows, mesh_count), 1) == picked).astype(BF16)
+
+    def pack_listed(whole, cap, first_chunk):
+        rows = n * SLOT
+        chunk = (iota((rows, LANES), 0) % SLOT) // cap - first_chunk
+        packed = jnp.zeros((rows, LANES), F32)
+        for j in range(whole.shape[1] // LANES):
+            packed = jnp.where(chunk == j, whole[:, j * LANES : (j + 1) * LANES], packed)
+        return packed.astype(BF16).reshape(n, SLOT, LANES)
+
+    def spread_listed(packed, cap):
+        rows = n * SLOT
+        packed = packed.reshape(rows, LANES)
         chunk = (iota((rows, LANES), 0) % SLOT) // cap
-        packed = jnp.zeros((rows, LANES), F32)
-        for j in range(chunks):
-            packed = jnp.where(chunk == j, whole[:, j * LANES : (j + 1) * LANES], packed)
-        packed = packed.astype(BF16).reshape(n, SLOT, LANES)
-        send[...] = packed
-        every(
-            n - 1,
-            lambda i: exchange(
-                send, recv, send_sem, recv_sem, lax.rem(me + i + 1, n), me
-            ).start(),
-        )
-        recv[me] = send[me]
-
-    def receive_listed(recv, send, send_sem, recv_sem, cap, weights):
-        def wait(i):
-            q = lax.rem(me + i + 1, n)
-            exchange(send, recv, send_sem, recv_sem, q, q).wait_recv()
-
-        every(n - 1, wait)
-        rows = n * SLOT
-        packed = recv[...].reshape(rows, LANES).astype(F32)
-        chunk = (iota((rows, LANES), 0) % SLOT) // cap
-        spread = jnp.concatenate(
+        return jnp.concatenate(
             [jnp.where(chunk == j, packed, 0.0) for j in range(chunks)], axis=1
         ).astype(BF16)
-        return dot(spread, weights).astype(BF16)
+
+    def half_listed(q, c, at, from_core):
+        return pltpu.make_async_remote_copy(
+            src_ref=send1.at[q],
+            dst_ref=recv1.at[from_core, at],
+            send_sem=a_send.at[c, q],
+            recv_sem=a_recv.at[from_core, at],
+            device_id={"dom": q, "feat": c},
+            device_id_type=MESH,
+        )
+
+    def whole_listed(q, at):
+        return exchange(send2, recv2, b_send, b_recv, q, at)
 
     def slot_key(cap):
         r = iota((1, n * SLOT), 1)
@@ -214,36 +217,75 @@
     sender_col, receiver_col = columns[:, 0:1], columns[:, 1:2]
     dsender_col, dreceiver_col = columns[:, 2:3], columns[:, 3:4]
 
-    arrived(0)
-    send_listed(nodes[...], lists[...], send1, recv1, a_send, a_recv)
-
+    own[0].wait()
+    half_nodes = nodes[:, pl.ds(pl.multiple_of(core * width, width), width)]
     mesh_cap = lists_in.shape[1] // n
     grid_cap = dlists_in.shape[1] // n
+    send1[...] = pack_listed(
+        dot(listed_rows(lists[...]), half_nodes), mesh_cap, core * (chunks // 2)
+    )
+    recv1[core, me] = send1[me]
+    node_lane = iota((edge_count, mesh_count), 1)
+    pick_sender = (node_lane == sender_col).astype(BF16)
+    pick_receiver = (node_lane == receiver_col).astype(BF16)
+
+    pl.semaphore_wait(barrier, 2 * n - 1)
+    far[0].start()
+    far[1].start()
+
+    def send_halves(i):
+        q = lax.rem(me + i + 1, n)
+        for c in range(2):
+            half_listed(q, c, me, core).start()
+
+    every(n - 1, send_halves)
+    half_listed(me, other, me, core).start()
+    for copy in far[2:]:
+        copy.start()
+
+    far[0].wait_recv()
     arrived(1)
     from_sender = dot(nodes[...], ef[latent : 2 * latent, :]).astype(BF16)
     from_receiver = dot(nodes[...], ef[2 * latent : 3 * latent, :]).astype(BF16)
-    node_lane = iota((edge_count, mesh_count), 1)
-    pick_sender = (node_lane == sender_col).astype(BF16)
-    pick_receiver = (node_lane == receiver_col).astype(BF16)
     pre = dot(pick_sender, from_sender) + dot(pick_receiver, from_receiver)
     arrived(2)
     pre = pre + dot(edges[...], ef[0:latent, :])
-    table = receive_listed(recv1, send1, a_send, a_recv, mesh_cap, ef[latent : 2 * latent, :])
     pick_slot = (slot_key(mesh_cap) == sender_col - mesh_count).astype(BF16)
+    gather = (iota((mesh_count, edge_count), 0) == receiver).astype(BF16)
+    arrived(4)
+    listed = listed_rows(dlists[...])
+    listed_gather = dot(listed, gather).astype(BF16)
+    listed_nodes = dot(listed, nodes[...])
+    listed_pre = dot(listed_nodes.astype(BF16), nf[0:latent, :])
+
+    def wait_halves(i):
+        q = lax.rem(me + i + 1, n)
+        for c in range(2):
+            half_listed(q, c, q, c).wait_recv()
+
+    every(n - 1, wait_halves)
+    half_listed(me, other, me, other).wait_recv()
+    packed = recv1[0].astype(F32) + recv1[1].astype(F32)
+    table = dot(spread_listed(packed, mesh_cap), ef[latent : 2 * latent, :]).astype(BF16)
     hidden = silu(pre + dot(pick_slot, table))
     arrived(3)
     message = (
         edges[...].astype(F32) + norm_scale(dot(hidden, es[...])) * eg[...]
     ).astype(BF16)
-    gather = (iota((mesh_count, edge_count), 0) == receiver).astype(BF16)
+
+    def update(before, first_pre, taken):
+        hidden = silu(first_pre + dot(taken, nf[latent : 2 * latent, :]))
+        return before + norm_scale(dot(hidden, ns[...])) * ng[...]
+
+    arrived(5)
+    listed_taken = dot(listed_gather, message).astype(BF16)
+    send2[...] = pack_listed(update(listed_nodes, listed_pre, listed_taken), grid_cap, 0)
+    every(n - 1, lambda i: whole_listed(lax.rem(me + i + 1, n), me).start())
+    recv2[me] = send2[me]
+
     collected = dot(gather, message).astype(BF16)
-
-    arrived(4)
-    hidden = silu(dot(nodes[...], nf[0:latent, :]) + dot(collected, nf[latent : 2 * latent, :]))
-    arrived(5)
-    updated = (nodes[...].astype(F32) + norm_scale(dot(hidden, ns[...])) * ng[...]).astype(BF16)
-    mesh_full[...] = updated
-    send_listed(updated, dlists[...], send2, recv2, b_send, b_recv)
+    node_pre = dot(nodes[...], nf[0:latent, :])
+    mesh_full[...] = update(nodes[...].astype(F32), node_pre, collected).astype(BF16)
     put_mesh = pltpu.make_async_copy(column_half(mesh_full, core), mesh_out, out_sem.at[0])
     put_mesh.start()
 
@@ -254,14 +296,21 @@
     pre = dot(links[...], df[0:latent, :]) + dot(pick_grid, from_grid)
     arrived(10)
     grid_pre = dot(grid[...], gf[0:latent, :])
-    table = receive_listed(recv2, send2, b_send, b_recv, grid_cap, df[latent : 2 * latent, :])
     pick_slot = (slot_key(grid_cap) == dsender_col).astype(BF16)
+    gather = (iota((grid_count, edge_count), 0) == dreceiver).astype(BF16)
+
+    def wait_whole(i):
+        q = lax.rem(me + i + 1, n)
+        whole_listed(q, q).wait_recv()
+
+    every(n - 1, wait_whole)
+    packed = recv2[...].astype(F32)
+    table = dot(spread_listed(packed, grid_cap), df[latent : 2 * latent, :]).astype(BF16)
     hidden = silu(pre + dot(pick_slot, table))
     arrived(9)
     message = (
         links[...].astype(F32) + norm_scale(dot(hidden, ds[...])) * dg[...]
     ).astype(BF16)
-    gather = (iota((grid_count, edge_count), 0) == dreceiver).astype(BF16)
     collected = dot(gather, message).astype(BF16)
 
     hidden = silu(grid_pre + dot(collected, gf[latent : 2 * latent, :]))
@@ -277,12 +326,32 @@
 
     def sent(i):
         q = lax.rem(me + i + 1, n)
-        exchange(send1, recv1, a_send, a_recv, q, q).wait_send()
-        exchange(send2, recv2, b_send, b_recv, q, q).wait_send()
+        for c in range(2):
+            half_listed(q, c, q, c).wait_send()
+        whole_listed(q, q).wait_send()
 
     every(n - 1, sent)
+    half_listed(me, other, me, other).wait_send()
     put_mesh.wait()
     put_grid.wait()
+
+
+def place(mesh_in, grid_in, mesh_out, grid_out, mesh_held, grid_held, sem):
+    take = (
+        pltpu.make_async_copy(mesh_in, mesh_held, sem.at[0]),
+        pltpu.make_async_copy(grid_in, grid_held, sem.at[1]),
+    )
+    put = (
+        pltpu.make_async_copy(mesh_held, mesh_out, sem.at[2]),
+        pltpu.make_async_copy(grid_held, grid_out, sem.at[3]),
+    )
+    for copy in take:
+        copy.start()
+    for first, second in zip(take, put):
+        first.wait()
+        second.start()
+    for copy in put:
+        copy.wait()
 
 
 def local(n, *args):
@@ -308,7 +377,7 @@
 
     slots = pltpu.VMEM((n, SLOT, LANES), BF16)
     dma = pltpu.SemaphoreType.DMA
-    return pl.pallas_call(
+    outs = pl.pallas_call(
         functools.partial(kernel, n),
         out_shape=(
             jax.ShapeDtypeStruct(args[0].shape, BF16),
@@ -323,16 +392,24 @@
             whole_columns(args[15]), whole_rows(args[16]), same(args[17]),
             whole_columns(args[18]), whole_rows(args[19]), same(args[20]),
             whole_columns(args[21]), whole_rows(args[22]), same(args[23]),
-            slots, slots, slots, slots,
+            slots, pltpu.VMEM((2, n, SLOT, LANES), BF16), slots, slots,
             whole_columns(args[0]), whole_columns(args[2]),
             dma((12,)), dma((12,)), dma((12,)), dma((10,)),
-            dma((n,)), dma((n,)), dma((n,)), dma((n,)), dma((2,)),
+            dma((2, n)), dma((2, n)), dma((n,)), dma((n,)), dma((2,)),
         ],
         compiler_params=pltpu.CompilerParams(
             collective_id=0, has_side_effects=True, vmem_limit_bytes=56 * 1024 * 1024
         ),
         name="layer",
     )(*args)
+    return pl.pallas_call(
+        place,
+        out_shape=tuple(jax.ShapeDtypeStruct(o.shape, o.dtype) for o in outs),
+        in_specs=[any_spec, any_spec],
+        out_specs=(any_spec, any_spec),
+        scratch_shapes=[same(outs[0]), same(outs[1]), dma((4,))],
+        name="place",
+    )(*outs)
 
 
 def solution(mesh):

time: 25.2 us -> 23.6 us (0.937)
  local copies, waits for them, and re-layouts: 2.26 us -> 0 us
  Pallas kernels: 22.1 us -> 22.8 us
    unnamed x4 -> x0, local copies, waits for them, and re-layouts: 2.26 us -> none
    pallas_call x0 -> x1, Pallas kernels: none -> 1.66 us  [local(): pl.pallas_call(place, out_shape=tuple((jax.ShapeDtypeStruct(o.shape, o.dt...]
    pallas_call x1, Pallas kernels: 22.1 us -> 21.1 us  [local(): pl.pallas_call(functools.partial(kernel, n), out_shape=(jax.ShapeDtypeStr...]
where the time goes in v2:
time: 23.6 us; the launch traced here: 23.4 us
  Pallas kernels  22.8 us (97%)
  between operations  0.65 us (3%)
    pallas_call x1, Pallas kernels, local(): pl.pallas_call(functools.partial(kernel, n), out_shape=(jax.ShapeDtypeStr...  21.1 us
    pallas_call x1, Pallas kernels, local(): pl.pallas_call(place, out_shape=tuple((jax.ShapeDtypeStruct(o.shape, o.dt...  1.66 us

profile of v2, /device:TPU:0, one launch (start us, length us, event | category | flops | bytes accessed | tf_op | source)
XLA Modules:
  0.0 23.4 jit_solution(10139428772820790771)
XLA Ops:
  0.6 21.1 %layer.1 = (bf16[256,256]{1,0:T(8,128)(2,1)}, bf16[256,256]{1,0:T(8,128)(2,1)}) custom-call(bf16[256,256]{1,0:T(8,128)(2,1)} %refs_0_.1, bf16[512,256]{1,0:T(8,128)(2,1)} %refs_1_.1, bf16[256,256]{1,0:T(8,128)(2,1)} %refs_2_.1, bf16[512,256]{1,0:T(8,128)(2,1)} %refs_3_.1, s32[1,512]{1,0:T(1,128)} %bitcast.8, s32[4]{0:T(128)} %refs_5_.1, s32[1,512]{1,0:T(1,128)} %bitcast.9, ...), custom_call_target="tpu_custom_call" | custom-call | tf_op jit(solution)/shard_map/layer/pallas_call | solution.py:380
  21.8 1.7 %place.1 = (bf16[256,256]{1,0:T(8,128)(2,1)}, bf16[256,256]{1,0:T(8,128)(2,1)}) custom-call(bf16[256,256]{1,0:T(8,128)(2,1)} %get-tuple-element.4.mesh_in, bf16[256,256]{1,0:T(8,128)(2,1)} %get-tuple-element.5.grid_in), custom_call_target="tpu_custom_call" | custom-call | tf_op jit(solution)/shard_map/place/pallas_call | solution.py:405
